TPU v7x, 32 devices: a whole 2x2x4 slice. The times are simulated.
32 devices in a mesh: dp: 8 (over y, x, core), tensor: 4 (over z).
Axes of the slice: x: 2, y: 2, z: 4, core: 2. Of those that a mesh axis runs over, the one named last changes fastest.
Arguments:
- hidden: bfloat16 [1024, 8192], P('dp', 'tensor')
- rotation: float32 [8192, 8192], P('dp', 'tensor'), may hold values from -0.0625 to 0.0625
- channel_scale: float32 [8192], P('tensor')
- lengths: int32 [16], P('dp'), may hold values from 16 to 64, as said below
Outputs:
- direction: float32 [8192, 8192], P('dp', 'tensor')
- loss: float32 [], replicated
Inputs may be any that keep to these rules, and one draw needn't show every extreme that they name: `lengths`: each sequence's valid length; some sequence is full in every draw.
All inputs are finite; a program needn't handle non-finite values.
Results may differ from a plain program's by a relative error of at most 0.00075.
The roundings to bfloat16 on the way count: a program that leaves them out, or rounds other values in their place, can miss the bound.
Values may be sent and summed in bfloat16 or wider, within the bound.
A program may use at most 128 MiB of HBM per device.

v0:
```python
import math
import jax
import jax.numpy as jnp
from jax import lax
from jax.sharding import PartitionSpec as P

D = 8192
SEQ = 64


def local(hidden, rotation, channel_scale, lengths):
    narrow_rotation = rotation.astype(jnp.bfloat16)
    features = lax.all_gather(hidden, "tensor", axis=1, tiled=True)
    column_blocks = lax.all_to_all(features, "dp", split_axis=1, concat_axis=0, tiled=True)
    partial = jnp.dot(column_blocks, narrow_rotation, preferred_element_type=jnp.float32)
    rotated = lax.psum_scatter(partial, "dp", scatter_dimension=0, tiled=True)
    scaled = rotated * channel_scale[None, :]
    token_square = lax.psum(jnp.sum(scaled * scaled, axis=1), "tensor")
    step_size = 4.0 * jnp.sqrt(token_square / D + 1e-06)[:, None]
    token_index = jnp.arange(hidden.shape[0], dtype=jnp.int32)
    position = token_index % SEQ
    sequence_index = token_index // SEQ
    sequence_count = lengths.shape[0]
    owners = sequence_index[:, None] == jnp.arange(sequence_count, dtype=jnp.int32)[None, :]
    inside = position[:, None] < lengths[None, :]
    live_mask = jnp.sum(jnp.where(owners & inside, 1.0, 0.0), axis=1).astype(jnp.float32)[:, None]
    angles = math.pi * scaled / step_size
    error_local = jnp.sum(live_mask * jnp.sin(angles) ** 2)
    count_local = jnp.sum(lengths).astype(jnp.float32) / lax.axis_size("tensor")
    error_slope = (
        live_mask * (math.pi / step_size) * jnp.sin(2.0 * angles) * channel_scale[None, :]
    ).astype(jnp.bfloat16)
    gradient = lax.dot_general(
        column_blocks,
        lax.all_gather(error_slope, "dp", axis=0, tiled=True),
        (((0,), (0,)), ((), ())),
        preferred_element_type=jnp.float32,
    )
    error_sum, count = lax.psum((error_local, count_local), ("dp", "tensor"))
    grad_square = lax.psum(jnp.sum(gradient * gradient), ("dp", "tensor"))
    direction = gradient / jnp.sqrt(grad_square / (D * D) + 1e-06)
    loss = error_sum / (D * count)
    return (direction, loss)


def solution(mesh):
    return jax.shard_map(
        local,
        mesh=mesh,
        in_specs=(P("dp", "tensor"), P("dp", "tensor"), P("tensor"), P("dp")),
        out_specs=(P("dp", "tensor"), P()),
        check_vma=False,
    )
```

profile of v0, /device:TPU:0, one launch (start us, length us, event | category | flops | bytes accessed | tf_op | source)
XLA Modules:
  0.0 305.9 jit_solution(8076852472374651479)
XLA Ops:
  7.2 0.0 all-gather.3.cloned.1.call-start
  7.2 2.0 copy.11
  9.3 0.0 all-gather.3.cloned.1.call-update
  9.3 0.0 reduce-scatter.2.cloned.1.call-start
  9.3 49.5 %all-gather.3.cloned.1.call-done = bf16[128,8192]{0,1:T(8,128)(2,1)} async-done(((bf16[128,2048]{0,1:T(8,128)(2,1)}), bf16[128,8192]{0,1:T(8,128)(2,1)}) %all-gather.3.cloned.1.call-update) | async-done | bytes 2097168 | tf_op jit(solution)/shard_map/all_gather | solution.py:13
  58.8 30.2 %all_to_all.19 = bf16[128,8,1024]{0,2,1:T(8,128)(2,1)S(1)} all-to-all(bf16[128,8,1024]{0,2,1:T(8,128)(2,1)} %bitcast.11), channel_id=1, replica_groups=mesh['dp'=8,'tensor'=4] {'dp'}, dimensions={1} | all-to-all | bytes 4194304 | tf_op jit(solution)/shard_map/all_to_all | solution.py:14
  89.0 2.6 copy.12
  91.6 11.9 %fusion = f32[1024,2048]{1,0:T(8,128)} fusion(bf16[1024,1024]{1,0:T(8,128)(2,1)} %bitcast.9, f32[1024,2048]{1,0:T(8,128)} %param.5), kind=kOutput, calls=%fused_computation.2 | convolution fusion | flops 4297064448 | bytes 18874368 | tf_op jit(solution)/shard_map/dot_general | solution.py:15
  103.6 0.0 copy-start.2
  103.6 0.0 copy-start.1
  103.6 0.0 copy-start
  103.6 0.0 reduce-scatter.2.cloned.1.call-update
  103.6 0.0 all-gather.5.cloned.1.call-start
  103.6 0.6 copy-done.2
  104.2 0.1 fusion.2
  104.3 67.6 %reduce-scatter.2.cloned.1.call-done = f32[128,2048]{1,0:T(8,128)} async-done(((f32[1024,2048]{1,0:T(8,128)}), f32[128,2048]{1,0:T(8,128)}) %reduce-scatter.2.cloned.1.call-update) | async-done | bytes 1048592 | tf_op jit(solution)/shard_map/reduce_scatter | solution.py:16
  171.9 0.0 copy-done.1
  171.9 1.4 multiply_reduce_fusion.2
  173.3 11.7 %psum.28 = f32[128]{0:T(128)S(1)} all-reduce(f32[128]{0:T(128)S(1)} %multiply_reduce_fusion.2), channel_id=1, replica_groups=mesh['dp'=8,'tensor'=4] {'tensor'}, use_global_device_ids=true, to_apply=%region_3.4 | all-reduce | flops 128 | bytes 1024 | tf_op jit(solution)/shard_map/psum | solution.py:18
  185.0 9.9 %multiply_reduce_fusion.1 = (f32[]{:T(128)}, bf16[128,2048]{1,0:T(8,128)(2,1)}) fusion(f32[128]{0:T(128)S(1)} %fusion.2, f32[128]{0:T(128)S(1)} %get-tuple-element.15, f32[128,2048]{1,0:T(8,128)} %reduce-scatter.2.cloned.1.call-done, f32[2048]{0:T(1024)S(1)} %copy-done.1, f32[128]{0:T(128)S(1)} %get-tuple-element.16), kind=kLoop, calls=%fused_computation.4 | loop fusion | flops 2621439 | bytes 1582596 | tf_op jit(solution)/shard_map/reduce_sum | solution.py:28
  194.9 0.0 all-gather.5.cloned.1.call-update
  195.0 0.6 reduce_sum.49
  196.2 32.9 %all-gather.5.cloned.1.call-done = bf16[1024,2048]{1,0:T(8,128)(2,1)} async-done(((bf16[128,2048]{1,0:T(8,128)(2,1)}), bf16[1024,2048]{1,0:T(8,128)(2,1)}) %all-gather.5.cloned.1.call-update) | async-done | bytes 4194320 | tf_op jit(solution)/shard_map/all_gather | solution.py:35
  229.0 0.0 copy-done
  229.1 10.1 %multiply_reduce_fusion = (f32[]{:T(128)}, f32[2048,1024]{1,0:T(8,128)}) fusion(bf16[1024,2048]{1,0:T(8,128)(2,1)} %all-gather.5.cloned.1.call-done, bf16[1024,1024]{1,0:T(8,128)(2,1)S(1)} %bitcast.10), kind=kOutput, calls=%fused_computation.1 | convolution fusion | flops 4299161600 | bytes 14680068 | tf_op jit(solution)/shard_map/dot_general | solution.py:33
  239.2 39.6 %all-reduce = (f32[]{:T(128)}, f32[]{:T(128)}, f32[]{:T(128)}) all-reduce(f32[]{:T(128)} %get-tuple-element.17, f32[]{:T(128)} %get-tuple-element.13, f32[]{:T(128)S(6)} %div.59), channel_id=1, replica_groups=mesh['dp'=8,'tensor'=4] {'dp','tensor'}, use_global_device_ids=true, to_apply=%region_5.6 | all-reduce | flops 3 | bytes 24 | tf_op jit(solution)/shard_map/psum | solution.py:40
  279.4 8.5 %divide_bitcast_fusion = f32[1024,2048]{0,1:T(8,128)} fusion(f32[2048,1024]{1,0:T(8,128)} %get-tuple-element.18, f32[]{:T(128)S(6)} %sqrt.7), kind=kLoop, calls=%fused_computation | loop fusion | flops 2097152 | bytes 16777220 | tf_op jit(solution)/shard_map/div | solution.py:41
  287.9 9.1 %copy.13 = f32[1024,2048]{1,0:T(8,128)} copy(f32[1024,2048]{0,1:T(8,128)} %divide_bitcast_fusion) | data formatting | bytes 16777216
  (2 shorter events, 0.0 us)
Async XLA Ops:
  7.2 51.6 %all-gather.3.cloned.1.call-start = ((), (), s32[]{:S(2)}) async-start(), calls=%async_computation.2 | async-start | bytes 2621440 | tf_op jit(solution)/shard_map/all_gather | solution.py:13
  9.3 162.6 %reduce-scatter.2.cloned.1.call-start = ((), (), s32[]{:S(2)}) async-start(), calls=%async_computation.3 | async-start | bytes 9437184 | tf_op jit(solution)/shard_map/reduce_scatter | solution.py:16
  103.6 0.7 copy-start.2
  103.6 68.4 %copy-start.1 = (f32[2048]{0:T(1024)S(1)}, f32[2048]{0:T(1024)}, u32[]{:S(2)}) copy-start(f32[2048]{0:T(1024)} %param.6) | copy-start | bytes 24580
  103.6 125.5 %copy-start = (bf16[8,128,1024]{2,1,0:T(8,128)(2,1)S(1)}, bf16[8,128,1024]{2,1,0:T(8,128)(2,1)}, u32[]{:S(2)}) copy-start(bf16[8,128,1024]{2,1,0:T(8,128)(2,1)} %copy.12) | copy-start | bytes 6291460
  103.6 125.5 %all-gather.5.cloned.1.call-start = ((), (), s32[]{:S(2)}) async-start(), calls=%async_computation.4 | async-start | bytes 4718592 | tf_op jit(solution)/shard_map/all_gather | solution.py:35
Sparse Core Ops, SparseCore 0:
  10.1 48.6 all-gather.2
  103.7 68.1 reduce-scatter.1
  195.1 33.9 all-gather.4
where the time goes:
time: 307 us; the launch traced here: 306 us
  waiting for transfers between devices  150 us (49%)
  blocking collectives  81.5 us (27%)
  matrix products  22 us (7%)
  other arithmetic  20.6 us (7%)
  between operations  17.3 us (6%)
  local copies, waits for them, and re-layouts  14.3 us (5%)
    reduce_scatter x1, waiting for transfers between devices, local(): rotated = lax.psum_scatter(partial, 'dp', scatter_dimension=0, tiled=True)  67.6 us
    all_gather x1, waiting for transfers between devices, local(): features = lax.all_gather(hidden, 'tensor', axis=1, tiled=True)  49.5 us
    psum x1, blocking collectives, local(): grad_square = lax.psum(jnp.sum(gradient * gradient), ('dp', 'tensor'))  39.6 us
    all_gather x1, waiting for transfers between devices, local(): lax.all_gather(error_slope, 'dp', axis=0, tiled=True)  32.9 us
    all_to_all x1, blocking collectives, local(): lax.all_to_all(features, 'dp', split_axis=1, concat_axis=0, tiled=True)  30.2 us
    dot_general x1, matrix products, local(): jnp.dot(column_blocks, narrow_rotation, preferred_element_type=jnp.float32)  11.9 us
    unnamed x8, local copies, waits for them, and re-layouts  11.7 us
    psum x1, blocking collectives, local(): token_square = lax.psum(jnp.sum(scaled * scaled, axis=1), 'tensor')  11.7 us
  transfers between devices with their start and end apart: 3, of which 3 were waited for; matrix products, arithmetic and copies ran while one was open for 0% of the time, Pallas kernels for 0%

commit v1 on v0

--- a/solution.py
+++ b/solution.py
@@ -10,7 +10,19 @@
 
 def local(hidden, rotation, channel_scale, lengths):
     narrow_rotation = rotation.astype(jnp.bfloat16)
-    features = lax.all_gather(hidden, "tensor", axis=1, tiled=True)
+    shares = lax.axis_size("tensor")
+    leaves = tuple(((c, (c + 1) % shares) for c in range(shares)))
+    h_now, local_out = ([hidden], [hidden])
+    block_list = tuple(((c, (c - 1) % shares) for c in range(shares)))
+    for _ in range(shares // 2):
+        before = lax.ppermute(h_now[-1], "tensor", perm=leaves)
+        h_now.append(before)
+    for _ in range((shares - 1) // 2):
+        oldest = lax.ppermute(local_out[-1], "tensor", perm=block_list)
+        local_out.append(oldest)
+    piece_next = jnp.concatenate([*h_now[::-1], *local_out[1:]], axis=1)
+    value_now = lax.axis_index("tensor")
+    features = jnp.roll(piece_next, (value_now - shares // 2) * hidden.shape[1], axis=1)
     column_blocks = lax.all_to_all(features, "dp", split_axis=1, concat_axis=0, tiled=True)
     partial = jnp.dot(column_blocks, narrow_rotation, preferred_element_type=jnp.float32)
     rotated = lax.psum_scatter(partial, "dp", scatter_dimension=0, tiled=True)

time: 307 us -> 290 us (0.945)
  waiting for transfers between devices: 150 us -> 136 us
  local copies, waits for them, and re-layouts: 14.3 us -> 5.15 us
  starting transfers between devices: 0.12 us -> 6.98 us
    all_gather x1 -> x0, waiting for transfers between devices: 49.5 us -> none  [local(): features = lax.all_gather(hidden, 'tensor', axis=1, tiled=True)]
    ppermute x0 -> x3, waiting for transfers between devices: none -> 34.3 us  [the longest x2 26.8 us: local(): before = lax.ppermute(h_now[-1], 'tensor', perm=leaves)]
    unnamed x8 -> x14, local copies, waits for them, and re-layouts: 11.7 us -> 2.34 us
    ppermute x0 -> x3, starting transfers between devices: none -> 6.9 us  [the longest x1 3.82 us: local(): oldest = lax.ppermute(local_out[-1], 'tensor', perm=block_list)]
  transfers between devices with their start and end apart: 3 -> 5, of which waited for: 3 -> 5; matrix products, arithmetic and copies ran while one was open for 0% -> 0% of each run, Pallas kernels for 0% -> 0%
where the time goes in v1:
time: 290 us
  waiting for transfers between devices  136 us (47%)
  blocking collectives  81.1 us (28%)
  matrix products  22.1 us (8%)
  other arithmetic  20.5 us (7%)
  between operations  17.8 us (6%)
  starting transfers between devices  6.98 us (2%)
  local copies, waits for them, and re-layouts  5.15 us (2%)
    reduce_scatter x1, waiting for transfers between devices, local(): rotated = lax.psum_scatter(partial, 'dp', scatter_dimension=0, tiled=True)  68.9 us
    psum x1, blocking collectives, local(): grad_square = lax.psum(jnp.sum(gradient * gradient), ('dp', 'tensor'))  39.6 us
    all_gather x1, waiting for transfers between devices, local(): lax.all_gather(error_slope, 'dp', axis=0, tiled=True)  32.9 us
    all_to_all x1, blocking collectives, local(): lax.all_to_all(features, 'dp', split_axis=1, concat_axis=0, tiled=True)  29.9 us
    ppermute x2, waiting for transfers between devices, local(): before = lax.ppermute(h_now[-1], 'tensor', perm=leaves)  26.8 us
    dot_general x1, matrix products, local(): jnp.dot(column_blocks, narrow_rotation, preferred_element_type=jnp.float32)  11.9 us
    psum x1, blocking collectives, local(): token_square = lax.psum(jnp.sum(scaled * scaled, axis=1), 'tensor')  11.7 us
    dot_general x1, matrix products, local(): lax.dot_general(column_blocks, lax.all_gather(error_slope, 'dp', axis=0,...  10.2 us
  transfers between devices with their start and end apart: 5, of which 5 were waited for; matrix products, arithmetic and copies ran while one was open for 0% of the time, Pallas kernels for 0%

profile of v1, /device:TPU:0, one launch (start us, length us, event | category | flops | bytes accessed | tf_op | source)
XLA Modules:
  0.0 289.7 jit_solution(11695082299080600296)
XLA Ops:
  7.2 0.0 reduce-scatter.2.cloned.1.call-start
  7.2 1.3 copy.11
  8.5 3.1 %collective-permute-start = (bf16[128,2048]{0,1:T(8,128)(2,1)S(1)}, bf16[128,2048]{0,1:T(8,128)(2,1)S(1)}, u32[]{:S(2)}, u32[]{:S(2)}) collective-permute-start(bf16[128,2048]{0,1:T(8,128)(2,1)S(1)} %copy.11), channel_id=1, source_target_pairs={{0,1},{1,2},{2,3},{3,0},{4,5},{5,6},{6,7},{7,4},{8,9},{9,10},{10,1... | collective-permute-start | bytes 1572872 | tf_op jit(solution)/shard_map/ppermute | solution.py:18
  11.6 13.9 %collective-permute-done = bf16[128,2048]{0,1:T(8,128)(2,1)S(1)} collective-permute-done((bf16[128,2048]{0,1:T(8,128)(2,1)S(1)}, bf16[128,2048]{0,1:T(8,128)(2,1)S(1)}, u32[]{:S(2)}, u32[]{:S(2)}) %collective-permute-start) | collective-permute-done | bytes 524320 | tf_op jit(solution)/shard_map/ppermute | solution.py:18
  25.6 3.8 %collective-permute-start.2 = (bf16[128,2048]{0,1:T(8,128)(2,1)S(1)}, bf16[128,2048]{0,1:T(8,128)(2,1)S(1)}, u32[]{:S(2)}, u32[]{:S(2)}) collective-permute-start(bf16[128,2048]{0,1:T(8,128)(2,1)S(1)} %copy.11), channel_id=1, source_target_pairs={{0,3},{1,0},{2,1},{3,2},{4,7},{5,4},{6,5},{7,6},{8,11},{9,8},{10,9... | collective-permute-start | bytes 1572872 | tf_op jit(solution)/shard_map/ppermute | solution.py:21
  29.4 12.8 %collective-permute-done.1 = bf16[128,2048]{0,1:T(8,128)(2,1)S(1)} collective-permute-done((bf16[128,2048]{0,1:T(8,128)(2,1)S(1)}, bf16[128,2048]{0,1:T(8,128)(2,1)S(1)}, u32[]{:S(2)}, u32[]{:S(2)}) %collective-permute-start.1) | collective-permute-done | bytes 524320 | tf_op jit(solution)/shard_map/ppermute | solution.py:18
  42.3 0.1 constant_dynamic-update-slice_fusion.6
  42.3 0.1 constant_dynamic-update-slice_fusion.5
  42.4 7.5 %collective-permute-done.2 = bf16[128,2048]{0,1:T(8,128)(2,1)S(1)} collective-permute-done((bf16[128,2048]{0,1:T(8,128)(2,1)S(1)}, bf16[128,2048]{0,1:T(8,128)(2,1)S(1)}, u32[]{:S(2)}, u32[]{:S(2)}) %collective-permute-start.2) | collective-permute-done | bytes 524320 | tf_op jit(solution)/shard_map/ppermute | solution.py:21
  49.9 0.1 constant_dynamic-update-slice_fusion.4
  50.0 0.1 constant_dynamic-update-slice_fusion.3
  50.0 0.1 constant_dynamic-update-slice_fusion.2
  50.1 0.1 constant_dynamic-update-slice_fusion.1
  50.2 0.1 constant_dynamic-update-slice_fusion
  50.3 0.1 constant_dynamic-slice_fusion
  50.4 29.9 %all_to_all.19 = bf16[128,8,1024]{0,2,1:T(8,128)(2,1)S(1)} all-to-all(bf16[128,8,1024]{0,2,1:T(8,128)(2,1)S(1)} %bitcast.6), channel_id=1, replica_groups=mesh['dp'=8,'tensor'=4] {'dp'}, dimensions={1} | all-to-all | bytes 4194304 | tf_op jit(solution)/shard_map/all_to_all | solution.py:26
  80.3 2.6 copy.15
  82.9 11.9 %fusion = f32[1024,2048]{1,0:T(8,128)} fusion(bf16[1024,1024]{1,0:T(8,128)(2,1)} %bitcast.8, f32[1024,2048]{1,0:T(8,128)} %param.5), kind=kOutput, calls=%fused_computation.2 | convolution fusion | flops 4297064448 | bytes 18874368 | tf_op jit(solution)/shard_map/dot_general | solution.py:27
  94.8 0.0 reduce-scatter.2.cloned.1.call-update
  94.9 0.0 all-gather.2.cloned.1.call-start
  94.9 0.6 copy-done.2
  95.5 0.1 fusion.2
  95.6 68.9 %reduce-scatter.2.cloned.1.call-done = f32[128,2048]{1,0:T(8,128)} async-done(((f32[1024,2048]{1,0:T(8,128)}), f32[128,2048]{1,0:T(8,128)}) %reduce-scatter.2.cloned.1.call-update) | async-done | bytes 1048592 | tf_op jit(solution)/shard_map/reduce_scatter | solution.py:28
  164.5 1.4 multiply_reduce_fusion.2
  165.9 11.7 %psum.28 = f32[128]{0:T(128)S(1)} all-reduce(f32[128]{0:T(128)S(1)} %multiply_reduce_fusion.2), channel_id=1, replica_groups=mesh['dp'=8,'tensor'=4] {'tensor'}, use_global_device_ids=true, to_apply=%region_3.4 | all-reduce | flops 128 | bytes 1024 | tf_op jit(solution)/shard_map/psum | solution.py:30
  177.6 9.9 %multiply_reduce_fusion.1 = (f32[]{:T(128)}, bf16[128,2048]{1,0:T(8,128)(2,1)}) fusion(f32[128]{0:T(128)S(1)} %fusion.2, f32[128]{0:T(128)S(1)} %get-tuple-element.7, f32[128,2048]{1,0:T(8,128)} %reduce-scatter.2.cloned.1.call-done, f32[2048]{0:T(1024)S(1)} %copy-done.1, f32[128]{0:T(128)S(1)} %get-tuple-element.8), kind=kLoop, calls=%fused_computation.4 | loop fusion | flops 2621439 | bytes 1582596 | tf_op jit(solution)/shard_map/reduce_sum | solution.py:40
  187.5 0.0 all-gather.2.cloned.1.call-update
  187.5 0.6 reduce_sum.49
  188.7 32.9 %all-gather.2.cloned.1.call-done = bf16[1024,2048]{1,0:T(8,128)(2,1)} async-done(((bf16[128,2048]{1,0:T(8,128)(2,1)}), bf16[1024,2048]{1,0:T(8,128)(2,1)}) %all-gather.2.cloned.1.call-update) | async-done | bytes 4194320 | tf_op jit(solution)/shard_map/all_gather | solution.py:47
  221.6 10.2 %multiply_reduce_fusion = (f32[]{:T(128)}, f32[1024,2048]{1,0:T(8,128)}) fusion(bf16[1024,1024]{1,0:T(8,128)(2,1)S(1)} %bitcast.9, bf16[1024,2048]{1,0:T(8,128)(2,1)} %all-gather.2.cloned.1.call-done), kind=kOutput, calls=%fused_computation | convolution fusion | flops 4299161600 | bytes 14680068 | tf_op jit(solution)/shard_map/dot_general | solution.py:45
  231.8 39.6 %all-reduce = (f32[]{:T(128)}, f32[]{:T(128)}, f32[]{:T(128)}) all-reduce(f32[]{:T(128)} %get-tuple-element.9, f32[]{:T(128)} %get-tuple-element.5, f32[]{:T(128)S(6)} %div.55), channel_id=1, replica_groups=mesh['dp'=8,'tensor'=4] {'dp','tensor'}, use_global_device_ids=true, to_apply=%region_5.6 | all-reduce | flops 3 | bytes 24 | tf_op jit(solution)/shard_map/psum | solution.py:52
  273.3 8.4 %broadcast_divide_fusion = f32[1024,2048]{1,0:T(8,128)} fusion(f32[1024,2048]{1,0:T(8,128)} %get-tuple-element.10, f32[]{:T(128)S(6)} %sqrt.7), kind=kLoop, calls=%fused_computation.1 | loop fusion | flops 2097152 | bytes 16777220 | tf_op jit(solution)/shard_map/div | solution.py:53
  (9 shorter events, 0.1 us)
Async XLA Ops:
  7.2 157.3 %reduce-scatter.2.cloned.1.call-start = ((), (), s32[]{:S(2)}) async-start(), calls=%async_computation.2 | async-start | bytes 9437184 | tf_op jit(solution)/shard_map/reduce_scatter | solution.py:28
  8.5 17.0 %collective-permute-start = (bf16[128,2048]{0,1:T(8,128)(2,1)S(1)}, bf16[128,2048]{0,1:T(8,128)(2,1)S(1)}, u32[]{:S(2)}, u32[]{:S(2)}) collective-permute-start(bf16[128,2048]{0,1:T(8,128)(2,1)S(1)} %copy.11), channel_id=1, source_target_pairs={{0,1},{1,2},{2,3},{3,0},{4,5},{5,6},{6,7},{7,4},{8,9},{9,10},{10,1... | collective-permute-start | bytes 1572872 | tf_op jit(solution)/shard_map/ppermute | solution.py:18
  25.6 16.7 %collective-permute-start.1 = (bf16[128,2048]{0,1:T(8,128)(2,1)S(1)}, bf16[128,2048]{0,1:T(8,128)(2,1)S(1)}, u32[]{:S(2)}, u32[]{:S(2)}) collective-permute-start(bf16[128,2048]{0,1:T(8,128)(2,1)S(1)} %collective-permute-done), channel_id=1, source_target_pairs={{0,1},{1,2},{2,3},{3,0},{4,5},{5,6},{6,7},{7,4},{8,9},{9,10},{10,1... | collective-permute-start | bytes 1572872 | tf_op jit(solution)/shard_map/ppermute | solution.py:18
  25.6 24.3 %collective-permute-start.2 = (bf16[128,2048]{0,1:T(8,128)(2,1)S(1)}, bf16[128,2048]{0,1:T(8,128)(2,1)S(1)}, u32[]{:S(2)}, u32[]{:S(2)}) collective-permute-start(bf16[128,2048]{0,1:T(8,128)(2,1)S(1)} %copy.11), channel_id=1, source_target_pairs={{0,3},{1,0},{2,1},{3,2},{4,7},{5,4},{6,5},{7,6},{8,11},{9,8},{10,9... | collective-permute-start | bytes 1572872 | tf_op jit(solution)/shard_map/ppermute | solution.py:21
  94.8 0.7 copy-start.2
  94.8 69.6 %copy-start.1 = (f32[2048]{0:T(1024)S(1)}, f32[2048]{0:T(1024)}, u32[]{:S(2)}) copy-start(f32[2048]{0:T(1024)} %param.6) | copy-start | bytes 24580
  94.8 126.8 %copy-start = (bf16[8,128,1024]{2,1,0:T(8,128)(2,1)S(1)}, bf16[8,128,1024]{2,1,0:T(8,128)(2,1)}, u32[]{:S(2)}) copy-start(bf16[8,128,1024]{2,1,0:T(8,128)(2,1)} %copy.15) | copy-start | bytes 6291460
  94.9 126.7 %all-gather.2.cloned.1.call-start = ((), (), s32[]{:S(2)}) async-start(), calls=%async_computation.3 | async-start | bytes 4718592 | tf_op jit(solution)/shard_map/all_gather | solution.py:47
Sparse Core Ops, SparseCore 0:
  95.0 69.4 reduce-scatter.1
  187.6 33.9 all-gather.1
